TPU v7x, 256 devices: a whole 4x4x8 slice. The times are simulated.
256 devices in a mesh: blk: 64 (over x, z, y_hi), col: 4 (over y_lo, core).
Axes of the slice: x: 4, y: 4 (y_hi: 2, y_lo: 2; y = y_hi * 2 + y_lo), z: 8, core: 2. Of those that a mesh axis runs over, the one named last changes fastest.
Arguments:
- node_features: bfloat16 [131072, 128], P(('blk', 'col')), may hold values from -6 to 6
- degree: int32 [131072], P(('blk', 'col')), may hold values from 1 to 8
- adjacency: bfloat16 [92160, 128, 128], P(('blk', 'col')), may hold values from -0.125 to 0.125
- tile_rows: int32 [92160], P(('blk', 'col')), may hold values from 0 to 15
- tile_cols: int32 [92160], P(('blk', 'col')), may hold values from 0 to 3
- counts: int32 [1280], P(('blk', 'col')), may hold values from 1 to 72, as said below
- weight: bfloat16 [128, 256], replicated, may hold values from -0.5 to 0.5
- bias_vector: float32 [256], replicated, may hold values from -3 to 3
- cotangent: bfloat16 [131072, 256], P(('blk', 'col')), may hold values from -6 to 6
Outputs:
- activations: bfloat16 [131072, 256], P(('blk', 'col'))
- grad_features: bfloat16 [131072, 128], P(('blk', 'col'))
- grad_weight: float32 [128, 256], replicated
- grad_bias: float32 [256], replicated
Inputs may be any that keep to these rules, and one draw needn't show every extreme that they name: `counts`: every draw has some pair with all 72 slots live.
All inputs are finite; a program needn't handle non-finite values.
Results may differ from a plain program's by a relative error of at most 0.012.
Values may be sent and summed in bfloat16 or wider, within the bound.
A program may use at most 128 MiB of HBM per device.

v0:
```python
import jax
import jax.numpy as jnp
from jax import lax
from jax.sharding import PartitionSpec as P


def from_behind(value, axis, by):
    length = lax.axis_size(axis)
    return lax.ppermute(value, axis, [(i, (i + by) % length) for i in range(length)])


def shortened(value):

    def short(part):
        return part.astype(jnp.bfloat16) if part.dtype == jnp.float32 else part

    return jax.tree.map(short, value)


def local(
    node_features, degree, adjacency, tile_rows, tile_cols, counts, weight, bias_vector, cotangent
):
    offset_count = counts.shape[0]
    reach_steps = (offset_count - 1) // 2
    tile_size = adjacency.shape[1]
    slot_count = adjacency.shape[0] // offset_count
    own_rows, features = node_features.shape
    own_tiles = own_rows // tile_size
    col_count = lax.axis_size("col")
    block_tiles = col_count * own_tiles
    live_slots = jnp.arange(slot_count)[None, :] < counts[:, None]
    adjacency = adjacency.reshape(offset_count, slot_count, tile_size, tile_size)
    adjacency = jnp.where(live_slots[:, :, None, None], adjacency, jnp.zeros_like(adjacency))
    dest_tiles = tile_rows.reshape(offset_count, slot_count)
    source_tiles = tile_cols.reshape(offset_count, slot_count)
    row_scale = lax.rsqrt(degree.astype(jnp.float32))
    source = (row_scale[:, None] * node_features.astype(jnp.float32)).astype(jnp.bfloat16)
    fetched = [source] * offset_count
    ahead_rows = source
    behind_rows = source
    for distance in range(1, reach_steps + 1):
        ahead_rows = from_behind(ahead_rows, "blk", -1)
        behind_rows = from_behind(behind_rows, "blk", 1)
        fetched[reach_steps + distance] = ahead_rows
        fetched[reach_steps - distance] = behind_rows
    picked = jnp.stack(
        [
            fetched[offset].reshape(own_tiles, tile_size, features)[source_tiles[offset]]
            for offset in range(offset_count)
        ]
    )
    products = jnp.einsum("ksrq,ksqf->ksrf", adjacency, picked, preferred_element_type=jnp.float32)
    block_sums = jax.ops.segment_sum(
        products.reshape(-1, tile_size, features), dest_tiles.reshape(-1), block_tiles
    )
    block_sums = block_sums.reshape(block_tiles * tile_size, features)
    sums = lax.psum_scatter(block_sums, "col", scatter_dimension=0, tiled=True)
    aggregated = (row_scale[:, None] * sums).astype(jnp.bfloat16)
    pre_act = jnp.dot(aggregated, weight, preferred_element_type=jnp.float32) + bias_vector
    gate_value = jax.nn.sigmoid(pre_act)
    activations = (pre_act * gate_value).astype(jnp.bfloat16)
    grad_pre = cotangent.astype(jnp.float32) * gate_value * (1.0 + pre_act * (1.0 - gate_value))
    grad_low = grad_pre.astype(jnp.bfloat16)
    weight_part = lax.dot_general(
        aggregated, grad_low, (((0,), (0,)), ((), ())), preferred_element_type=jnp.float32
    )
    bias_part = jnp.sum(grad_pre, axis=0)
    weight_sum, bias_sum = lax.psum((weight_part, bias_part), ("blk", "col"))
    norm_factor = float(own_rows * lax.axis_size("blk") * col_count) ** (-0.5)
    grad_rows = lax.dot_general(
        grad_low, weight, (((1,), (1,)), ((), ())), preferred_element_type=jnp.float32
    )
    grad_hidden = (row_scale[:, None] * grad_rows).astype(jnp.bfloat16)
    block_grad = lax.all_gather(grad_hidden, "col", axis=0, tiled=True)
    picked_grad = block_grad.reshape(block_tiles, tile_size, features)[dest_tiles]
    back_terms = jnp.einsum(
        "ksrq,ksrf->ksqf", adjacency, picked_grad, preferred_element_type=jnp.float32
    )
    target_ids = jnp.arange(offset_count)[:, None] * own_tiles + source_tiles
    outgoing = jax.ops.segment_sum(
        back_terms.reshape(-1, tile_size, features),
        target_ids.reshape(-1),
        offset_count * own_tiles,
    )
    outgoing = outgoing.reshape(offset_count, own_rows, features)
    total_back = outgoing[reach_steps]
    carry_up = jnp.zeros((own_rows, features), jnp.float32)
    carry_down = jnp.zeros((own_rows, features), jnp.float32)
    for distance in range(reach_steps, 0, -1):
        carry_up = from_behind(shortened(carry_up + outgoing[reach_steps + distance]), "blk", 1)
        carry_down = from_behind(
            shortened(carry_down + outgoing[reach_steps - distance]), "blk", -1
        )
    total_back = total_back + carry_up + carry_down
    grad_features = (row_scale[:, None] * total_back).astype(jnp.bfloat16)
    return (activations, grad_features, weight_sum * norm_factor, bias_sum * norm_factor)


def solution(mesh):
    return jax.shard_map(
        local,
        mesh=mesh,
        in_specs=(
            P(("blk", "col"), None),
            P(("blk", "col")),
            P(("blk", "col"), None, None),
            P(("blk", "col")),
            P(("blk", "col")),
            P(("blk", "col")),
            P(),
            P(),
            P(("blk", "col"), None),
        ),
        out_specs=(P(("blk", "col"), None), P(("blk", "col"), None), P(), P()),
        check_vma=False,
    )
```

profile of v0, /device:TPU:8, one launch (start us, length us, event | category | flops | bytes accessed | tf_op | source)
XLA Modules:
  0.0 485.8 jit_solution(10293052520780361430)
XLA Ops:
  7.2 0.0 copy-start
  7.2 0.0 reduce-scatter.2.cloned.1.call-start
  7.2 0.7 convert_rsqrt_fusion
  7.9 1.0 multiply_convert_fusion.2
  9.0 2.4 collective-permute-start
  11.3 7.6 %collective-permute-start.2 = (bf16[512,128]{1,0:T(8,128)(2,1)S(1)}, bf16[512,128]{1,0:T(8,128)(2,1)S(1)}, u32[]{:S(2)}, u32[]{:S(2)}) collective-permute-start(bf16[512,128]{1,0:T(8,128)(2,1)S(1)} %multiply_convert_fusion.2), channel_id=1, source_target_pairs={{0,252},{4,0},{8,4},{12,8},{16,12},{20,16},{24,20},{28,24},{32,28}... | collective-permute-start | bytes 393224 | tf_op jit(solution)/shard_map/ppermute | solution.py:9
  18.9 0.9 compare_select_fusion.1
  19.8 0.7 iota_compare_fusion
  20.6 1.7 collective-permute-done
  22.3 0.0 collective-permute-start.1
  22.3 16.3 %copy.15 = bf16[5,72,128,128]{2,3,1,0:T(8,128)(2,1)} copy(bf16[5,72,128,128]{3,2,1,0:T(8,128)(2,1)} %bitcast.57) | data formatting | bytes 23592960 | tf_op jit(solution)/shard_map/reshape | solution.py:32
  38.6 1.0 gather_fusion.2
  39.6 2.4 gather_fusion.1
  42.1 0.0 collective-permute-done.2
  42.1 2.4 gather_fusion.3
  44.5 7.7 %collective-permute-start.3 = (bf16[512,128]{1,0:T(8,128)(2,1)S(1)}, bf16[512,128]{1,0:T(8,128)(2,1)S(1)}, u32[]{:S(2)}, u32[]{:S(2)}) collective-permute-start(bf16[512,128]{1,0:T(8,128)(2,1)S(1)} %collective-permute-done.2), channel_id=1, source_target_pairs={{0,252},{4,0},{8,4},{12,8},{16,12},{20,16},{24,20},{28,24},{32,28}... | collective-permute-start | bytes 393224 | tf_op jit(solution)/shard_map/ppermute | solution.py:9
  52.2 0.0 collective-permute-done.1
  52.3 2.5 gather_fusion
  54.7 2.0 bitcast_dynamic-update-slice_fusion.4
  56.7 2.1 bitcast_dynamic-update-slice_fusion.3
  58.8 0.3 bitcast_dynamic-update-slice_fusion.2
  59.1 0.3 bitcast_dynamic-update-slice_fusion.1
  59.4 0.0 collective-permute-done.3
  59.5 4.3 copy-done.3
  63.8 1.0 gather_fusion.4
  64.8 1.6 bitcast_dynamic-update-slice_fusion
  66.4 14.5 %fusion.1 = f32[5,72,128,128]{3,2,1,0:T(8,128)} fusion(bf16[5,72,128,128]{3,2,1,0:T(8,128)(2,1)} %bitcast_dynamic-update-slice_fusion, bf16[5,72,128,128]{2,3,1,0:T(8,128)(2,1)} %copy.15, pred[5,72]{1,0:T(8,128)(4,1)S(1)} %iota_compare_fusion), kind=kOutput, calls=%fused_computation.10 | convolution fusion | flops 1515847680 | bytes 47186280 | tf_op jit(solution)/shard_map/ksrq,ksqf->ksrf/dot_general | solution.py:52
  81.0 0.1 broadcast_in_dim.42
  81.1 0.0 copy-start.6
  81.1 0.0 copy-start.8
  81.1 0.0 copy-start.9
  81.1 47.9 %scatter_fusion = f32[16,128,128]{2,1,0:T(8,128)S(1)} fusion(f32[16,128,128]{2,1,0:T(8,128)S(1)} %broadcast_in_dim.42, s32[360]{0:T(512)S(1)} %copy-done.7, f32[360,128,128]{2,1,0:T(8,128)} %bitcast.50), kind=kCustom, calls=%fused_computation.6 | custom fusion | flops 5898240 | bytes 70780320 | tf_op jit(solution)/shard_map/scatter-add | solution.py:53
  129.0 1.0 copy-done.2
  130.0 0.0 reduce-scatter.2.cloned.1.call-update
  130.0 0.0 all-reduce.2.cloned.1.call-start
  130.1 0.1 reshape.136
  130.2 0.1 reshape.180
  130.3 0.1 add.86
  130.3 0.1 add.87
  130.4 16.4 %reduce-scatter.2.cloned.1.call-done = f32[512,128]{1,0:T(8,128)} async-done(((f32[2048,128]{1,0:T(8,128)}), f32[512,128]{1,0:T(8,128)}) %reduce-scatter.2.cloned.1.call-update) | async-done | bytes 262160 | tf_op jit(solution)/shard_map/reduce_scatter | solution.py:57
  146.9 2.1 fusion.15
  149.0 0.2 fusion.4
  149.2 7.6 %all_gather.3 = bf16[2048,128]{1,0:T(8,128)(2,1)S(1)} all-gather(bf16[512,128]{1,0:T(8,128)(2,1)S(1)} %fusion.4), channel_id=1, replica_groups=mesh['blk'=64,'col'=4] {'col'}, dimensions={0}, use_global_device_ids=true | all-gather | bytes 655360 | tf_op jit(solution)/shard_map/all_gather | solution.py:74
  156.8 11.1 %gather_fusion.5 = bf16[360,128,128]{2,1,0:T(8,128)(2,1)} fusion(bf16[16,128,128]{2,1,0:T(8,128)(2,1)S(1)} %bitcast.48, s32[1024]{0:T(1024)S(1)} %pad_clamp_fusion), kind=kCustom, calls=%fused_computation.5 | custom fusion | bytes 23594400 | tf_op jit(solution)/shard_map/gather | solution.py:75
  167.8 15.3 %fusion = f32[5,72,128,128]{3,2,1,0:T(8,128)} fusion(bf16[5,72,128,128]{3,2,1,0:T(8,128)(2,1)} %bitcast.52, bf16[5,72,128,128]{2,3,1,0:T(8,128)(2,1)} %copy.15, pred[5,72]{1,0:T(8,128)(4,1)S(1)} %iota_compare_fusion), kind=kOutput, calls=%fused_computation.9 | convolution fusion | flops 1515847680 | bytes 47186280 | tf_op jit(solution)/shard_map/ksrq,ksrf->ksqf/dot_general | solution.py:76
  183.1 0.1 broadcast_in_dim.50
  183.2 0.0 copy-start.1
  183.2 47.9 %scatter_fusion.1 = f32[20,128,128]{2,1,0:T(8,128)S(1)} fusion(f32[20,128,128]{2,1,0:T(8,128)S(1)} %broadcast_in_dim.50, s32[360]{0:T(512)S(1)} %add.88, f32[360,128,128]{2,1,0:T(8,128)} %bitcast.49), kind=kCustom, calls=%fused_computation.7 | custom fusion | flops 5898240 | bytes 70780320 | tf_op jit(solution)/shard_map/scatter-add | solution.py:80
  231.1 0.1 fusion.16
  231.1 0.1 convert.4
  231.3 1.0 fusion.10
  232.2 0.0 all-reduce.2.cloned.1.call-update
  232.3 2.3 collective-permute-start.4
  234.6 5.5 %collective-permute-start.6 = (bf16[512,128]{1,0:T(8,128)(2,1)S(1)}, bf16[512,128]{1,0:T(8,128)(2,1)S(1)}, u32[]{:S(2)}, u32[]{:S(2)}) collective-permute-start(bf16[512,128]{1,0:T(8,128)(2,1)S(1)} %bitcast.58), channel_id=1, source_target_pairs={{0,252},{4,0},{8,4},{12,8},{16,12},{20,16},{24,20},{28,24},{32,28}... | collective-permute-start | bytes 393224 | tf_op jit(solution)/shard_map/ppermute | solution.py:9
  240.1 73.4 %psum.15 = f32[256]{0:T(256)S(1)} all-reduce(f32[256]{0:T(256)S(1)} %get-tuple-element.4), channel_id=1, replica_groups=mesh['blk'=64,'col'=4] {'blk','col'}, use_global_device_ids=true, to_apply=%region_5.6 | all-reduce | flops 256 | bytes 2048 | tf_op jit(solution)/shard_map/psum | solution.py:68
  313.6 0.6 broadcast_multiply_fusion.1
  314.2 2.1 collective-permute-start.5
  316.3 0.0 collective-permute-done.6
  316.3 5.8 %collective-permute-start.7 = (bf16[512,128]{1,0:T(8,128)(2,1)S(1)}, bf16[512,128]{1,0:T(8,128)(2,1)S(1)}, u32[]{:S(2)}, u32[]{:S(2)}) collective-permute-start(bf16[512,128]{1,0:T(8,128)(2,1)S(1)} %fusion.5), channel_id=1, source_target_pairs={{0,252},{4,0},{8,4},{12,8},{16,12},{20,16},{24,20},{28,24},{32,28}... | collective-permute-start | bytes 393224 | tf_op jit(solution)/shard_map/ppermute | solution.py:9
  322.1 154.5 %all-reduce.2.cloned.1.call-done = f32[128,256]{1,0:T(8,128)} async-done(((f32[128,256]{1,0:T(8,128)}), f32[128,256]{1,0:T(8,128)}) %all-reduce.2.cloned.1.call-update) | async-done | bytes 131088 | tf_op jit(solution)/shard_map/psum | solution.py:68
  476.6 1.6 broadcast_multiply_fusion
  478.2 0.0 collective-permute-done.5
  478.2 0.0 collective-permute-done.7
  478.2 0.8 fusion.9
  (25 shorter events, 0.2 us)
Async XLA Ops:
  7.2 139.7 %copy-start = (bf16[128,256]{1,0:T(8,128)(2,1)S(1)}, bf16[128,256]{1,0:T(8,128)(2,1)}, u32[]{:S(2)}) copy-start(bf16[128,256]{1,0:T(8,128)(2,1)} %param.15) | copy-start | bytes 196612
  7.2 139.7 %reduce-scatter.2.cloned.1.call-start = ((), (), s32[]{:S(2)}) async-start(), calls=%async_computation.1 | async-start | bytes 1310720 | tf_op jit(solution)/shard_map/reduce_scatter | solution.py:57
  9.0 13.4 %collective-permute-start = (bf16[512,128]{1,0:T(8,128)(2,1)S(1)}, bf16[512,128]{1,0:T(8,128)(2,1)S(1)}, u32[]{:S(2)}, u32[]{:S(2)}) collective-permute-start(bf16[512,128]{1,0:T(8,128)(2,1)S(1)} %multiply_convert_fusion.2), channel_id=1, source_target_pairs={{0,4},{4,8},{8,12},{12,16},{16,20},{20,24},{24,28},{28,32},{32,36}... | collective-permute-start | bytes 393224 | tf_op jit(solution)/shard_map/ppermute | solution.py:9
  11.3 30.8 %collective-permute-start.2 = (bf16[512,128]{1,0:T(8,128)(2,1)S(1)}, bf16[512,128]{1,0:T(8,128)(2,1)S(1)}, u32[]{:S(2)}, u32[]{:S(2)}) collective-permute-start(bf16[512,128]{1,0:T(8,128)(2,1)S(1)} %multiply_convert_fusion.2), channel_id=1, source_target_pairs={{0,252},{4,0},{8,4},{12,8},{16,12},{20,16},{24,20},{28,24},{32,28}... | collective-permute-start | bytes 393224 | tf_op jit(solution)/shard_map/ppermute | solution.py:9
  22.3 29.9 %collective-permute-start.1 = (bf16[512,128]{1,0:T(8,128)(2,1)S(1)}, bf16[512,128]{1,0:T(8,128)(2,1)S(1)}, u32[]{:S(2)}, u32[]{:S(2)}) collective-permute-start(bf16[512,128]{1,0:T(8,128)(2,1)S(1)} %collective-permute-done), channel_id=1, source_target_pairs={{0,4},{4,8},{8,12},{12,16},{16,20},{20,24},{24,28},{28,32},{32,36}... | collective-permute-start | bytes 393224 | tf_op jit(solution)/shard_map/ppermute | solution.py:9
  44.5 14.9 %collective-permute-start.3 = (bf16[512,128]{1,0:T(8,128)(2,1)S(1)}, bf16[512,128]{1,0:T(8,128)(2,1)S(1)}, u32[]{:S(2)}, u32[]{:S(2)}) collective-permute-start(bf16[512,128]{1,0:T(8,128)(2,1)S(1)} %collective-permute-done.2), channel_id=1, source_target_pairs={{0,252},{4,0},{8,4},{12,8},{16,12},{20,16},{24,20},{28,24},{32,28}... | collective-permute-start | bytes 393224 | tf_op jit(solution)/shard_map/ppermute | solution.py:9
  54.7 4.4 copy-start.4
  59.4 4.3 copy-start.3
  66.4 14.6 %copy-start.7 = (s32[360]{0:T(512)S(1)}, s32[360]{0:T(512)}, u32[]{:S(2)}) copy-start(s32[360]{0:T(512)} %param.12) | copy-start | bytes 4324
  81.1 49.3 %copy-start.6 = (s32[360]{0:T(512)S(1)}, s32[360]{0:T(512)}, u32[]{:S(2)}) copy-start(s32[360]{0:T(512)} %param.13) | copy-start | bytes 4324
  81.1 65.8 %copy-start.8 = (bf16[512,256]{1,0:T(8,128)(2,1)S(1)}, bf16[512,256]{1,0:T(8,128)(2,1)}, u32[]{:S(2)}) copy-start(bf16[512,256]{1,0:T(8,128)(2,1)} %param.17) | copy-start | bytes 786436
  81.1 65.8 %copy-start.9 = (f32[256]{0:T(256)S(1)}, f32[256]{0:T(256)}, u32[]{:S(2)}) copy-start(f32[256]{0:T(256)} %param.16) | copy-start | bytes 3076
  129.0 1.0 copy-start.2
  130.0 346.6 %all-reduce.2.cloned.1.call-start = ((), (), s32[]{:S(2)}) async-start(), calls=%async_computation.2 | async-start | bytes 262144 | tf_op jit(solution)/shard_map/psum | solution.py:68
  183.2 48.1 %copy-start.5 = (f32[512,128]{1,0:T(8,128)S(1)}, f32[512,128]{1,0:T(8,128)}, u32[]{:S(2)}) copy-start(f32[512,128]{1,0:T(8,128)} %reduce-scatter.2.cloned.1.call-done) | copy-start | bytes 786436
  183.2 295.8 %copy-start.1 = (bf16[128,256]{1,0:T(8,128)(2,1)S(1)}, bf16[128,256]{1,0:T(8,128)(2,1)}, u32[]{:S(2)}) copy-start(bf16[128,256]{1,0:T(8,128)(2,1)} %param.15) | copy-start | bytes 196612
  232.3 81.8 %collective-permute-start.4 = (bf16[512,128]{1,0:T(8,128)(2,1)S(1)}, bf16[512,128]{1,0:T(8,128)(2,1)S(1)}, u32[]{:S(2)}, u32[]{:S(2)}) collective-permute-start(bf16[512,128]{1,0:T(8,128)(2,1)S(1)} %bitcast.59), channel_id=1, source_target_pairs={{0,4},{4,8},{8,12},{12,16},{16,20},{20,24},{24,28},{28,32},{32,36}... | collective-permute-start | bytes 393224 | tf_op jit(solution)/shard_map/ppermute | solution.py:9
  234.6 81.6 %collective-permute-start.6 = (bf16[512,128]{1,0:T(8,128)(2,1)S(1)}, bf16[512,128]{1,0:T(8,128)(2,1)S(1)}, u32[]{:S(2)}, u32[]{:S(2)}) collective-permute-start(bf16[512,128]{1,0:T(8,128)(2,1)S(1)} %bitcast.58), channel_id=1, source_target_pairs={{0,252},{4,0},{8,4},{12,8},{16,12},{20,16},{24,20},{28,24},{32,28}... | collective-permute-start | bytes 393224 | tf_op jit(solution)/shard_map/ppermute | solution.py:9
  314.2 164.0 %collective-permute-start.5 = (bf16[512,128]{1,0:T(8,128)(2,1)S(1)}, bf16[512,128]{1,0:T(8,128)(2,1)S(1)}, u32[]{:S(2)}, u32[]{:S(2)}) collective-permute-start(bf16[512,128]{1,0:T(8,128)(2,1)S(1)} %fusion.6), channel_id=1, source_target_pairs={{0,4},{4,8},{8,12},{12,16},{16,20},{20,24},{24,28},{28,32},{32,36}... | collective-permute-start | bytes 393224 | tf_op jit(solution)/shard_map/ppermute | solution.py:9
  316.3 161.9 %collective-permute-start.7 = (bf16[512,128]{1,0:T(8,128)(2,1)S(1)}, bf16[512,128]{1,0:T(8,128)(2,1)S(1)}, u32[]{:S(2)}, u32[]{:S(2)}) collective-permute-start(bf16[512,128]{1,0:T(8,128)(2,1)S(1)} %fusion.5), channel_id=1, source_target_pairs={{0,252},{4,0},{8,4},{12,8},{16,12},{20,16},{24,20},{28,24},{32,28}... | collective-permute-start | bytes 393224 | tf_op jit(solution)/shard_map/ppermute | solution.py:9
Sparse Core Ops, SparseCore 0:
  130.2 16.6 reduce-scatter.1
  232.4 244.1 all-reduce.1
where the time goes:
time: 488 us; the launch traced here: 486 us
  waiting for transfers between devices  173 us (35%)
  other arithmetic  102 us (21%)
  blocking collectives  81 us (17%)
  local copies, waits for them, and re-layouts  48.9 us (10%)
  starting transfers between devices  33.5 us (7%)
  matrix products  33.1 us (7%)
  between operations  14.3 us (3%)
    psum x1, waiting for transfers between devices, local(): weight_sum, bias_sum = lax.psum((weight_part, bias_part), ('blk', 'col'))  155 us
    psum x1, blocking collectives, local(): weight_sum, bias_sum = lax.psum((weight_part, bias_part), ('blk', 'col'))  73.4 us
    scatter-add x1, other arithmetic, local(): jax.ops.segment_sum(products.reshape(-1, tile_size, features), dest_tiles...  47.9 us
    scatter-add x1, other arithmetic, local(): jax.ops.segment_sum(back_terms.reshape(-1, tile_size, features), target_i...  47.9 us
    ppermute x8, starting transfers between devices, from_behind(): lax.ppermute(value, axis, [(i, (i + by) % length) for i in range(length)])  33.4 us
    reduce_scatter x1, waiting for transfers between devices, local(): sums = lax.psum_scatter(block_sums, 'col', scatter_dimension=0, tiled=True)  16.4 us
    reshape x1, local copies, waits for them, and re-layouts, local(): adjacency.reshape(offset_count, slot_count, tile_size, tile_size)  16.3 us
    dot_general x1, matrix products, local(): jnp.einsum('ksrq,ksrf->ksqf', adjacency, picked_grad, preferred_element_t...  15.3 us
  transfers between devices with their start and end apart: 10, of which 3 were waited for; matrix products, arithmetic and copies ran while one was open for 7% of the time, Pallas kernels for 0%

commit v1 on v0

--- a/solution.py
+++ b/solution.py
@@ -65,7 +65,7 @@
         aggregated, grad_low, (((0,), (0,)), ((), ())), preferred_element_type=jnp.float32
     )
     bias_part = jnp.sum(grad_pre, axis=0)
-    weight_sum, bias_sum = lax.psum((weight_part, bias_part), ("blk", "col"))
+    weight_sum, bias_sum = lax.psum(lax.psum((weight_part, bias_part), "col"), "blk")
     norm_factor = float(own_rows * lax.axis_size("blk") * col_count) ** (-0.5)
     grad_rows = lax.dot_general(
         grad_low, weight, (((1,), (1,)), ((), ())), preferred_element_type=jnp.float32

time: 488 us -> 1060 us (2.17)
  waiting for transfers between devices: 173 us -> 634 us
  blocking collectives: 81 us -> 195 us
    psum x1 -> x2, waiting for transfers between devices: 155 us -> 616 us  [the longest x1 616 us: local(): lax.psum(lax.psum((weight_part, bias_part), 'col'), 'blk')]
    psum x1 -> x2, blocking collectives: 73.4 us -> 188 us  [the longest x1 181 us: local(): lax.psum(lax.psum((weight_part, bias_part), 'col'), 'blk')]
  transfers between devices with their start and end apart: 10 -> 11, of which waited for: 3 -> 3; matrix products, arithmetic and copies ran while one was open for 7% -> 3% of each run, Pallas kernels for 0% -> 0%
where the time goes in v1:
time: 1060 us
  waiting for transfers between devices  634 us (60%)
  blocking collectives  195 us (18%)
  other arithmetic  102 us (10%)
  local copies, waits for them, and re-layouts  48.9 us (5%)
  starting transfers between devices  33.5 us (3%)
  matrix products  33.2 us (3%)
  between operations  14 us (1%)
    psum x1, waiting for transfers between devices, local(): lax.psum(lax.psum((weight_part, bias_part), 'col'), 'blk')  616 us
    psum x1, blocking collectives, local(): lax.psum(lax.psum((weight_part, bias_part), 'col'), 'blk')  181 us
    scatter-add x1, other arithmetic, local(): jax.ops.segment_sum(products.reshape(-1, tile_size, features), dest_tiles...  47.9 us
    scatter-add x1, other arithmetic, local(): jax.ops.segment_sum(back_terms.reshape(-1, tile_size, features), target_i...  47.9 us
    ppermute x8, starting transfers between devices, from_behind(): lax.ppermute(value, axis, [(i, (i + by) % length) for i in range(length)])  33.4 us
  transfers between devices with their start and end apart: 11, of which 3 were waited for; matrix products, arithmetic and copies ran while one was open for 3% of the time, Pallas kernels for 0%

profile of v1, /device:TPU:8, one launch (start us, length us, event | category | flops | bytes accessed | tf_op | source)
XLA Modules:
  0.0 1061.0 jit_solution(12903194084266064070)
XLA Ops:
  7.2 0.0 copy-start
  7.2 0.0 reduce-scatter.2.cloned.1.call-start
  7.2 0.7 convert_rsqrt_fusion
  7.9 1.0 multiply_convert_fusion.2
  9.0 2.4 collective-permute-start
  11.3 7.6 collective-permute-start.2
  18.9 0.9 compare_select_fusion.1
  19.8 0.7 iota_compare_fusion
  20.6 1.7 collective-permute-done
  22.3 0.0 collective-permute-start.1
  22.3 16.3 %copy.15 = bf16[5,72,128,128]{2,3,1,0:T(8,128)(2,1)} copy(bf16[5,72,128,128]{3,2,1,0:T(8,128)(2,1)} %bitcast.57) | data formatting | bytes 23592960 | tf_op jit(solution)/shard_map/reshape | solution.py:32
  38.6 1.0 gather_fusion.2
  39.6 2.4 gather_fusion.1
  42.0 0.0 collective-permute-done.2
  42.0 2.4 gather_fusion.3
  44.5 7.7 collective-permute-start.3
  52.2 0.0 collective-permute-done.1
  52.2 2.5 gather_fusion
  54.7 2.0 bitcast_dynamic-update-slice_fusion.4
  56.7 2.1 bitcast_dynamic-update-slice_fusion.3
  58.8 0.3 bitcast_dynamic-update-slice_fusion.2
  59.1 0.3 bitcast_dynamic-update-slice_fusion.1
  59.4 4.3 copy-done.3
  63.7 1.0 gather_fusion.4
  64.7 1.6 bitcast_dynamic-update-slice_fusion
  66.4 14.6 %fusion.1 = f32[5,72,128,128]{3,2,1,0:T(8,128)} fusion(bf16[5,72,128,128]{3,2,1,0:T(8,128)(2,1)} %bitcast_dynamic-update-slice_fusion, bf16[5,72,128,128]{2,3,1,0:T(8,128)(2,1)} %copy.15, pred[5,72]{1,0:T(8,128)(4,1)S(1)} %iota_compare_fusion), kind=kOutput, calls=%fused_computation.10 | convolution fusion | flops 1515847680 | bytes 47186280 | tf_op jit(solution)/shard_map/ksrq,ksqf->ksrf/dot_general | solution.py:52
  81.0 0.1 broadcast_in_dim.42
  81.1 0.0 copy-start.6
  81.1 0.0 copy-start.8
  81.1 0.0 copy-start.9
  81.1 47.9 %scatter_fusion = f32[16,128,128]{2,1,0:T(8,128)S(1)} fusion(f32[16,128,128]{2,1,0:T(8,128)S(1)} %broadcast_in_dim.42, s32[360]{0:T(512)S(1)} %copy-done.7, f32[360,128,128]{2,1,0:T(8,128)} %bitcast.50), kind=kCustom, calls=%fused_computation.6 | custom fusion | flops 5898240 | bytes 70780320 | tf_op jit(solution)/shard_map/scatter-add | solution.py:53
  129.1 1.0 copy-done.2
  130.0 0.0 reduce-scatter.2.cloned.1.call-update
  130.0 0.0 all-reduce.3.cloned.1.call-start
  130.1 0.1 reshape.136
  130.2 0.1 reshape.180
  130.3 0.1 add.90
  130.3 0.1 add.91
  130.4 16.4 %reduce-scatter.2.cloned.1.call-done = f32[512,128]{1,0:T(8,128)} async-done(((f32[2048,128]{1,0:T(8,128)}), f32[512,128]{1,0:T(8,128)}) %reduce-scatter.2.cloned.1.call-update) | async-done | bytes 262160 | tf_op jit(solution)/shard_map/reduce_scatter | solution.py:57
  146.9 2.1 fusion.15
  149.0 0.2 fusion.4
  149.2 7.6 all_gather.3
  156.8 11.0 %gather_fusion.5 = bf16[360,128,128]{2,1,0:T(8,128)(2,1)} fusion(bf16[16,128,128]{2,1,0:T(8,128)(2,1)S(1)} %bitcast.48, s32[1024]{0:T(1024)S(1)} %pad_clamp_fusion), kind=kCustom, calls=%fused_computation.5 | custom fusion | bytes 23594400 | tf_op jit(solution)/shard_map/gather | solution.py:75
  167.8 15.3 %fusion = f32[5,72,128,128]{3,2,1,0:T(8,128)} fusion(bf16[5,72,128,128]{3,2,1,0:T(8,128)(2,1)} %bitcast.52, bf16[5,72,128,128]{2,3,1,0:T(8,128)(2,1)} %copy.15, pred[5,72]{1,0:T(8,128)(4,1)S(1)} %iota_compare_fusion), kind=kOutput, calls=%fused_computation.9 | convolution fusion | flops 1515847680 | bytes 47186280 | tf_op jit(solution)/shard_map/ksrq,ksrf->ksqf/dot_general | solution.py:76
  183.1 0.1 broadcast_in_dim.50
  183.2 0.0 copy-start.1
  183.2 47.9 %scatter_fusion.1 = f32[20,128,128]{2,1,0:T(8,128)S(1)} fusion(f32[20,128,128]{2,1,0:T(8,128)S(1)} %broadcast_in_dim.50, s32[360]{0:T(512)S(1)} %add.92, f32[360,128,128]{2,1,0:T(8,128)} %bitcast.49), kind=kCustom, calls=%fused_computation.7 | custom fusion | flops 5898240 | bytes 70780320 | tf_op jit(solution)/shard_map/scatter-add | solution.py:80
  231.1 0.1 fusion.16
  231.2 0.1 convert.4
  231.3 1.0 fusion.10
  232.3 0.0 all-reduce.3.cloned.1.call-update
  232.3 0.0 all-reduce.5.cloned.1.call-start
  232.4 2.4 collective-permute-start.4
  234.8 5.4 collective-permute-start.6
  240.2 7.0 psum.30
  247.2 180.6 %psum.31 = f32[256]{0:T(256)S(1)} all-reduce(f32[256]{0:T(256)S(1)} %psum.30), channel_id=1, replica_groups=mesh['blk'=64,'col'=4] {'blk'}, use_global_device_ids=true, to_apply=%region_7.8 | all-reduce | flops 256 | bytes 2048 | tf_op jit(solution)/shard_map/psum | solution.py:68
  427.8 0.6 broadcast_multiply_fusion.1
  428.4 0.1 collective-permute-start.5
  428.5 0.0 all-reduce.3.cloned.1.call-done
  428.5 0.0 all-reduce.5.cloned.1.call-update
  428.6 7.8 collective-permute-start.7
  436.4 615.7 %all-reduce.5.cloned.1.call-done = f32[128,256]{1,0:T(8,128)} async-done(((f32[128,256]{1,0:T(8,128)}), f32[128,256]{1,0:T(8,128)}) %all-reduce.5.cloned.1.call-update) | async-done | bytes 131088 | tf_op jit(solution)/shard_map/psum | solution.py:68
  1052.1 1.6 broadcast_multiply_fusion
  1053.7 0.8 fusion.9
  (29 shorter events, 0.2 us)
Async XLA Ops:
  7.2 139.7 %copy-start = (bf16[128,256]{1,0:T(8,128)(2,1)S(1)}, bf16[128,256]{1,0:T(8,128)(2,1)}, u32[]{:S(2)}) copy-start(bf16[128,256]{1,0:T(8,128)(2,1)} %param.15) | copy-start | bytes 196612
  7.2 139.7 %reduce-scatter.2.cloned.1.call-start = ((), (), s32[]{:S(2)}) async-start(), calls=%async_computation.1 | async-start | bytes 1310720 | tf_op jit(solution)/shard_map/reduce_scatter | solution.py:57
  9.0 13.4 %collective-permute-start = (bf16[512,128]{1,0:T(8,128)(2,1)S(1)}, bf16[512,128]{1,0:T(8,128)(2,1)S(1)}, u32[]{:S(2)}, u32[]{:S(2)}) collective-permute-start(bf16[512,128]{1,0:T(8,128)(2,1)S(1)} %multiply_convert_fusion.2), channel_id=1, source_target_pairs={{0,4},{4,8},{8,12},{12,16},{16,20},{20,24},{24,28},{28,32},{32,36}... | collective-permute-start | bytes 393224 | tf_op jit(solution)/shard_map/ppermute | solution.py:9
  11.3 30.7 %collective-permute-start.2 = (bf16[512,128]{1,0:T(8,128)(2,1)S(1)}, bf16[512,128]{1,0:T(8,128)(2,1)S(1)}, u32[]{:S(2)}, u32[]{:S(2)}) collective-permute-start(bf16[512,128]{1,0:T(8,128)(2,1)S(1)} %multiply_convert_fusion.2), channel_id=1, source_target_pairs={{0,252},{4,0},{8,4},{12,8},{16,12},{20,16},{24,20},{28,24},{32,28}... | collective-permute-start | bytes 393224 | tf_op jit(solution)/shard_map/ppermute | solution.py:9
  22.3 29.9 %collective-permute-start.1 = (bf16[512,128]{1,0:T(8,128)(2,1)S(1)}, bf16[512,128]{1,0:T(8,128)(2,1)S(1)}, u32[]{:S(2)}, u32[]{:S(2)}) collective-permute-start(bf16[512,128]{1,0:T(8,128)(2,1)S(1)} %collective-permute-done), channel_id=1, source_target_pairs={{0,4},{4,8},{8,12},{12,16},{16,20},{20,24},{24,28},{28,32},{32,36}... | collective-permute-start | bytes 393224 | tf_op jit(solution)/shard_map/ppermute | solution.py:9
  44.5 14.9 %collective-permute-start.3 = (bf16[512,128]{1,0:T(8,128)(2,1)S(1)}, bf16[512,128]{1,0:T(8,128)(2,1)S(1)}, u32[]{:S(2)}, u32[]{:S(2)}) collective-permute-start(bf16[512,128]{1,0:T(8,128)(2,1)S(1)} %collective-permute-done.2), channel_id=1, source_target_pairs={{0,252},{4,0},{8,4},{12,8},{16,12},{20,16},{24,20},{28,24},{32,28}... | collective-permute-start | bytes 393224 | tf_op jit(solution)/shard_map/ppermute | solution.py:9
  54.7 4.4 copy-start.4
  59.4 4.3 copy-start.3
  66.4 14.7 %copy-start.7 = (s32[360]{0:T(512)S(1)}, s32[360]{0:T(512)}, u32[]{:S(2)}) copy-start(s32[360]{0:T(512)} %param.12) | copy-start | bytes 4324
  81.1 49.3 %copy-start.6 = (s32[360]{0:T(512)S(1)}, s32[360]{0:T(512)}, u32[]{:S(2)}) copy-start(s32[360]{0:T(512)} %param.13) | copy-start | bytes 4324
  81.1 65.8 %copy-start.8 = (bf16[512,256]{1,0:T(8,128)(2,1)S(1)}, bf16[512,256]{1,0:T(8,128)(2,1)}, u32[]{:S(2)}) copy-start(bf16[512,256]{1,0:T(8,128)(2,1)} %param.17) | copy-start | bytes 786436
  81.1 65.8 %copy-start.9 = (f32[256]{0:T(256)S(1)}, f32[256]{0:T(256)}, u32[]{:S(2)}) copy-start(f32[256]{0:T(256)} %param.16) | copy-start | bytes 3076
  129.0 1.0 copy-start.2
  130.0 298.5 %all-reduce.3.cloned.1.call-start = ((), (), s32[]{:S(2)}) async-start(), calls=%async_computation.2 | async-start | bytes 262144 | tf_op jit(solution)/shard_map/psum | solution.py:68
  183.2 48.1 %copy-start.5 = (f32[512,128]{1,0:T(8,128)S(1)}, f32[512,128]{1,0:T(8,128)}, u32[]{:S(2)}) copy-start(f32[512,128]{1,0:T(8,128)} %reduce-scatter.2.cloned.1.call-done) | copy-start | bytes 786436
  183.2 871.2 %copy-start.1 = (bf16[128,256]{1,0:T(8,128)(2,1)S(1)}, bf16[128,256]{1,0:T(8,128)(2,1)}, u32[]{:S(2)}) copy-start(bf16[128,256]{1,0:T(8,128)(2,1)} %param.15) | copy-start | bytes 196612
  232.3 819.8 %all-reduce.5.cloned.1.call-start = ((), (), s32[]{:S(2)}) async-start(), calls=%async_computation.3 | async-start | bytes 262144 | tf_op jit(solution)/shard_map/psum | solution.py:68
  232.4 196.0 %collective-permute-start.4 = (bf16[512,128]{1,0:T(8,128)(2,1)S(1)}, bf16[512,128]{1,0:T(8,128)(2,1)S(1)}, u32[]{:S(2)}, u32[]{:S(2)}) collective-permute-start(bf16[512,128]{1,0:T(8,128)(2,1)S(1)} %bitcast.59), channel_id=1, source_target_pairs={{0,4},{4,8},{8,12},{12,16},{16,20},{20,24},{24,28},{28,32},{32,36}... | collective-permute-start | bytes 393224 | tf_op jit(solution)/shard_map/ppermute | solution.py:9
  234.8 193.8 %collective-permute-start.6 = (bf16[512,128]{1,0:T(8,128)(2,1)S(1)}, bf16[512,128]{1,0:T(8,128)(2,1)S(1)}, u32[]{:S(2)}, u32[]{:S(2)}) collective-permute-start(bf16[512,128]{1,0:T(8,128)(2,1)S(1)} %bitcast.58), channel_id=1, source_target_pairs={{0,252},{4,0},{8,4},{12,8},{16,12},{20,16},{24,20},{28,24},{32,28}... | collective-permute-start | bytes 393224 | tf_op jit(solution)/shard_map/ppermute | solution.py:9
  428.4 625.2 %collective-permute-start.5 = (bf16[512,128]{1,0:T(8,128)(2,1)S(1)}, bf16[512,128]{1,0:T(8,128)(2,1)S(1)}, u32[]{:S(2)}, u32[]{:S(2)}) collective-permute-start(bf16[512,128]{1,0:T(8,128)(2,1)S(1)} %fusion.6), channel_id=1, source_target_pairs={{0,4},{4,8},{8,12},{12,16},{16,20},{20,24},{24,28},{28,32},{32,36}... | collective-permute-start | bytes 393224 | tf_op jit(solution)/shard_map/ppermute | solution.py:9
  428.6 625.0 %collective-permute-start.7 = (bf16[512,128]{1,0:T(8,128)(2,1)S(1)}, bf16[512,128]{1,0:T(8,128)(2,1)S(1)}, u32[]{:S(2)}, u32[]{:S(2)}) collective-permute-start(bf16[512,128]{1,0:T(8,128)(2,1)S(1)} %fusion.5), channel_id=1, source_target_pairs={{0,252},{4,0},{8,4},{12,8},{16,12},{20,16},{24,20},{28,24},{32,28}... | collective-permute-start | bytes 393224 | tf_op jit(solution)/shard_map/ppermute | solution.py:9
Sparse Core Ops, SparseCore 0:
  130.2 16.6 reduce-scatter.1
  232.4 41.8 all-reduce.2
  428.7 623.3 all-reduce.4
